TPU v7x, 32 devices: a whole 2x2x4 slice. The times are simulated.
32 devices in a mesh: row: 4 (over z), col: 8 (over y, x, core).
Axes of the slice: x: 2, y: 2, z: 4, core: 2. Of those that a mesh axis runs over, the one named last changes fastest.
Arguments:
- right_sides: float32 [16, 1024, 1024], P(None, 'row', 'col'), may hold values from -6 to 6
- inverse_first: float32 [1024, 1024], P(None, 'row'), may hold values from -1.4 to 1.4, as said below
- inverse_second: float32 [1024, 1024], P(None, 'row'), may hold values from -1.4 to 1.4, as said below
- column_first: float32 [15, 1024, 1024], P(None, 'row', 'col'), may hold values from -0.1875 to 0.1875
- column_second: float32 [14, 1024, 1024], P(None, 'row', 'col'), may hold values from -0.1875 to 0.1875
Outputs:
- solutions: float32 [2, 1024, 1024], P(None, None, 'col')
- updated_sides: float32 [16, 1024, 1024], P(None, 'row', 'col')
Inputs may be any that keep to these rules, and one draw needn't show every extreme that they name: `inverse_first`: lower triangular; diagonal entries between 0.6 and 1.4. `inverse_second`: lower triangular; diagonal entries between 0.6 and 1.4.
All inputs are finite; a program needn't handle non-finite values.
Results may differ from a plain program's by a relative error of at most 0.000084.
Values sent between devices are 32-bit elements; how exact they have to be, the bound alone decides.
A program may use at most 128 MiB of HBM per device.

v0:
```python
import jax
import jax.numpy as jnp
from jax import lax
from jax.sharding import PartitionSpec as P

HIGHEST = lax.Precision.HIGHEST


def apply_inverse(inverse, rhs_block):
    local_product = jnp.dot(
        inverse, rhs_block, precision=HIGHEST, preferred_element_type=jnp.float32
    )
    return lax.psum(local_product, "row")


def fold_panel(fragment, solved):
    return jnp.einsum(
        "bij,jr->bir", fragment, solved, precision=HIGHEST, preferred_element_type=jnp.float32
    )


def update_rows(factor_panel, solved):
    return fold_panel(lax.all_gather(factor_panel, "col", axis=2, tiled=True), solved)


def on_device(right_sides, inverse_first, inverse_second, column_first, column_second):
    solved_first = apply_inverse(inverse_first, right_sides[0])
    after_first = right_sides[1:] - update_rows(column_first, solved_first)
    solved_second = apply_inverse(inverse_second, after_first[0])
    remainder = after_first[1:] - update_rows(column_second, solved_second)
    updated_sides = jnp.concatenate([right_sides[:1], after_first[:1], remainder], axis=0)
    solutions = jnp.stack([solved_first, solved_second])
    return (solutions, updated_sides)


def solution(mesh):
    placed = (
        P(None, "row", "col"),
        P(None, "row"),
        P(None, "row"),
        P(None, "row", "col"),
        P(None, "row", "col"),
    )
    return jax.shard_map(
        on_device,
        mesh=mesh,
        in_specs=placed,
        out_specs=(P(None, None, "col"), P(None, "row", "col")),
        check_vma=False,
    )
```

profile of v0, /device:TPU:8, one launch (start us, length us, event | category | flops | bytes accessed | tf_op | source)
XLA Modules:
  0.0 219.5 jit_solution(17699556091123239549)
XLA Ops:
  8.0 0.0 copy-start
  8.0 0.0 all-reduce.3.cloned.1.call-start
  8.1 1.2 copy-done
  9.2 2.7 %fusion.2 = f32[1024,128]{1,0:T(8,128)} fusion(f32[1024,256]{1,0:T(8,128)S(1)} %copy-done, f32[16,256,128]{2,1,0:T(8,128)} %param.5), kind=kOutput, calls=%fused_computation.7 | convolution fusion | flops 402653184 | bytes 1703936 | tf_op jit(solution)/shard_map/dot_general | solution.py:10
  11.9 0.0 all-reduce.3.cloned.1.call-update
  11.9 0.0 all-gather.3.cloned.1.call-start
  12.0 0.5 all-gather.3.cloned.1.call-update
  12.5 0.0 all-gather.5.cloned.1.call-start
  12.6 0.5 all-gather.5.cloned.1.call-update
  13.1 0.0 slice-start
  13.1 0.0 all-reduce.5.cloned.1.call-start
  13.2 1.5 slice-done
  14.7 1.8 copy.19
  16.4 35.0 %all-reduce.3.cloned.1.call-done = f32[1024,128]{1,0:T(8,128)} async-done(((f32[1024,128]{1,0:T(8,128)}), f32[1024,128]{1,0:T(8,128)}) %all-reduce.3.cloned.1.call-update) | async-done | bytes 524304 | tf_op jit(solution)/shard_map/psum | solution.py:13
  51.4 52.4 %all-gather.3.cloned.1.call-done = f32[15,256,1024]{2,1,0:T(8,128)} async-done(((f32[15,256,128]{2,1,0:T(8,128)}), f32[15,256,1024]{2,1,0:T(8,128)}) %all-gather.3.cloned.1.call-update) | async-done | bytes 15728656 | tf_op jit(solution)/shard_map/all_gather | solution.py:23
  103.8 0.0 copy-start.1
  103.8 21.5 %bitcast_subtract_fusion = f32[15,256,128]{1,2,0:T(8,128)S(1)} fusion(f32[15,256,128]{1,2,0:T(8,128)} %copy.19, f32[15,256,1024]{2,1,0:T(8,128)} %all-gather.3.cloned.1.call-done, f32[1024,128]{1,0:T(8,128)} %all-reduce.3.cloned.1.call-done), kind=kOutput, calls=%fused_computation.1 | convolution fusion | flops 6040289280 | bytes 20185088 | tf_op jit(solution)/shard_map/bij,jr->bir/dot_general | solution.py:17
  125.2 0.0 copy-done.1
  125.2 0.0 slice-start.1
  125.3 1.8 convolution_bitcast_fusion
  127.0 0.0 all-reduce.5.cloned.1.call-update
  127.1 0.0 slice-done.1
  127.1 0.1 copy.18
  127.2 62.0 %all-gather.5.cloned.1.call-done = f32[14,256,1024]{2,1,0:T(8,128)} async-done(((f32[14,256,128]{2,1,0:T(8,128)}), f32[14,256,1024]{2,1,0:T(8,128)}) %all-gather.5.cloned.1.call-update) | async-done | bytes 14680080 | tf_op jit(solution)/shard_map/all_gather | solution.py:23
  189.2 0.0 all-reduce.5.cloned.1.call-done
  189.2 18.6 %slice_subtract_fusion = f32[14,256,128]{1,2,0:T(8,128)S(1)} fusion(f32[15,256,128]{1,2,0:T(8,128)S(1)} %bitcast_subtract_fusion, f32[14,256,1024]{2,1,0:T(8,128)} %all-gather.5.cloned.1.call-done, f32[1024,128]{1,0:T(8,128)} %all-reduce.5.cloned.1.call-done), kind=kOutput, calls=%fused_computation.2 | convolution fusion | flops 5637603328 | bytes 18874368 | tf_op jit(solution)/shard_map/bij,jr->bir/dot_general | solution.py:17
  207.8 0.1 pad_maximum_fusion
  208.0 1.8 copy.12
  209.8 2.2 %pad_maximum_fusion.1 = f32[2,1024,128]{2,1,0:T(8,128)} fusion(f32[1,1024,128]{2,1,0:T(8,128)} %bitcast.26, f32[1,1024,128]{2,1,0:T(8,128)} %bitcast.25), kind=kLoop, calls=%fused_computation.4 | loop fusion | flops 262144 | bytes 2097152 | tf_op jit(solution)/shard_map/stack | solution.py:32
  (1 shorter events, 0.0 us)
Async XLA Ops:
  8.0 1.2 copy-start
  8.0 43.4 %all-reduce.3.cloned.1.call-start = ((), (), s32[]{:S(2)}) async-start(), calls=%async_computation | async-start | bytes 1048576 | tf_op jit(solution)/shard_map/psum | solution.py:13
  11.9 91.8 %all-gather.3.cloned.1.call-start = ((), (), s32[]{:S(2)}) async-start(), calls=%async_computation.1 | async-start | bytes 17694720 | tf_op jit(solution)/shard_map/all_gather | solution.py:23
  12.5 176.7 %all-gather.5.cloned.1.call-start = ((), (), s32[]{:S(2)}) async-start(), calls=%async_computation.3 | async-start | bytes 16515072 | tf_op jit(solution)/shard_map/all_gather | solution.py:23
  13.1 1.6 slice-start
  13.1 176.1 %all-reduce.5.cloned.1.call-start = ((), (), s32[]{:S(2)}) async-start(), calls=%async_computation.2 | async-start | bytes 1048576 | tf_op jit(solution)/shard_map/psum | solution.py:13
  103.8 21.5 %copy-start.1 = (f32[1024,256]{1,0:T(8,128)S(1)}, f32[1024,256]{1,0:T(8,128)}, u32[]{:S(2)}) copy-start(f32[1024,256]{1,0:T(8,128)} %param.7) | copy-start | bytes 3145732
  125.2 1.8 slice-start.1
Sparse Core Ops, SparseCore 0:
  12.1 39.2 all-reduce.2
  127.2 38.1 all-reduce.4
Sparse Core Ops, SparseCore 1:
  14.3 89.4 all-gather.2
  105.5 83.7 all-gather.4
where the time goes:
time: 221 us; the launch traced here: 219 us
  waiting for transfers between devices  150 us (68%)
  matrix products  44.5 us (20%)
  between operations  15.6 us (7%)
  local copies, waits for them, and re-layouts  6.37 us (3%)
  other arithmetic  2.37 us (1%)
    all_gather x2, waiting for transfers between devices, update_rows(): lax.all_gather(factor_panel, 'col', axis=2, tiled=True)  114 us
    dot_general x2, matrix products, fold_panel(): jnp.einsum('bij,jr->bir', fragment, solved, precision=HIGHEST, preferred_...  40.1 us
    psum x2, waiting for transfers between devices, apply_inverse(): return lax.psum(local_product, 'row')  35 us
    unnamed x7, local copies, waits for them, and re-layouts  4.86 us
    dot_general x2, matrix products, apply_inverse(): jnp.dot(inverse, rhs_block, precision=HIGHEST, preferred_element_type=jnp...  4.46 us
  transfers between devices with their start and end apart: 4, of which 3 were waited for; matrix products, arithmetic and copies ran while one was open for 11% of the time, Pallas kernels for 0%

commit v1 on v0

--- a/solution.py
+++ b/solution.py
@@ -1,9 +1,332 @@
+import functools
+
 import jax
 import jax.numpy as jnp
 from jax import lax
+from jax.experimental import pallas as pl
+from jax.experimental.pallas import tpu as pltpu
 from jax.sharding import PartitionSpec as P
 
 HIGHEST = lax.Precision.HIGHEST
+MESH = pl.DeviceIdType.MESH
+F32 = jnp.float32
+BF16 = jnp.bfloat16
+
+
+def split(value):
+    high = value.astype(BF16)
+    low = (value - high.astype(F32)).astype(BF16)
+    return high, low
+
+
+def product(a_high, a_low, b_high, b_low):
+    dot = functools.partial(jnp.dot, preferred_element_type=F32)
+    return dot(a_high, b_high) + (dot(a_high, b_low) + dot(a_low, b_high))
+
+
+def kernel(
+    rows, cols,
+    sides, inv_one, inv_two, c_one, c_two,
+    solved_out, sides_out,
+    acc, inv, c1, c2, partial, partial_in, solved, other_x, other_y,
+    op_high, op_low, outgoing, incoming, share_in,
+    local_sem, g_send, g_recv, f_send, f_recv, o_send, o_recv,
+    p_send, p_recv, b_send, b_recv, e_send, e_recv, r_send, r_recv, w_sem,
+):
+    nb, tile, lanes = sides.shape
+    pairs = (nb - 2) // 2
+    z, c = lax.axis_index("row"), lax.axis_index("col")
+    core, x, y = lax.rem(c, 2), lax.rem(c // 2, 2), c // 4
+    by_x, by_y, sibling = c + 2 - 4 * x, c + 4 - 8 * y, c + 1 - 2 * core
+    slot_x, slot_y = 2 * x + core, 2 * y + core
+    from_x, from_y = 2 * (1 - x) + core, 2 * (1 - y) + core
+
+    def remote(src, dst, send, recv, device):
+        return pltpu.make_async_remote_copy(
+            src_ref=src, dst_ref=dst, send_sem=send, recv_sem=recv,
+            device_id=device, device_id_type=MESH)
+
+    load_zero = pltpu.make_async_copy(sides.at[0], acc.at[0], local_sem.at[0])
+    load_inv1 = pltpu.make_async_copy(inv_one, inv.at[0], local_sem.at[1])
+    load_inv2 = pltpu.make_async_copy(inv_two, inv.at[1], local_sem.at[2])
+    load_rest = pltpu.make_async_copy(
+        sides.at[pl.ds(1, nb - 1)], acc.at[pl.ds(1, nb - 1)], local_sem.at[3])
+    runs = [
+        (c_one, c1, 0, 1, slot_x),
+        (c_one, c1, 1, pairs, slot_x),
+        (c_two, c2, 0, pairs, slot_x),
+        (c_one, c1, 1 + pairs, pairs, slot_y),
+        (c_two, c2, pairs, pairs, slot_y),
+    ]
+    own = [
+        pltpu.make_async_copy(
+            src.at[pl.ds(at, n)], dst.at[pl.ds(at, n), slot], local_sem.at[4 + k])
+        for k, (src, dst, at, n, slot) in enumerate(runs)]
+    to_sibling = [
+        remote(src.at[pl.ds(at, n)], dst.at[pl.ds(at, n), slot],
+               o_send.at[k], o_recv.at[k], (z, sibling))
+        for k, (src, dst, at, n, slot) in enumerate(runs)]
+    load_zero.start()
+    load_inv1.start()
+
+    barrier = pltpu.get_barrier_semaphore()
+    peers = [(z, by_x), (z, by_y), (z, sibling)]
+    peers += [(lax.rem(z + d, rows), c) for d in range(1, rows)]
+    for peer in peers:
+        pl.semaphore_signal(barrier, inc=1, device_id=peer, device_id_type=MESH)
+    load_rest.start()
+    load_inv2.start()
+    for copy in own:
+        copy.start()
+    pl.semaphore_wait(barrier, len(peers))
+
+    def gather(src, dst, k, base, along_x):
+        slot, device = (slot_x, by_x) if along_x else (slot_y, by_y)
+        return remote(src.at[k], dst.at[k, slot],
+                      g_send.at[base + k], g_recv.at[base + k], (z, device))
+
+    def forward(dst, k, base, along_x):
+        slot = from_x if along_x else from_y
+        return remote(dst.at[k, slot], dst.at[k, slot],
+                      f_send.at[base + k], f_recv.at[base + k], (z, sibling))
+
+    second = nb - 1
+
+    def of_pair(p, make):
+        return [make(c_one, c1, 1 + p, 0, True), make(c_one, c1, 1 + pairs + p, 0, False),
+                make(c_two, c2, p, second, True), make(c_two, c2, pairs + p, second, False)]
+
+    def gather_pair(p):
+        return of_pair(p, gather)
+
+    def forward_pair(p):
+        return of_pair(p, lambda src, dst, k, base, along: forward(dst, k, base, along))
+
+    def start_gathers(first, last):
+        @pl.loop(first, last)
+        def _(p):
+            for copy in gather_pair(p):
+                copy.start()
+
+    def pass_on(first, last):
+        @pl.loop(first, last)
+        def _(p):
+            for arrived, copy in zip(gather_pair(p), forward_pair(p)):
+                arrived.wait_recv()
+                copy.start()
+
+    head = gather(c_one, c1, 0, 0, True)
+    head_forward = forward(c1, 0, 0, True)
+    head.start()
+    to_sibling[0].start()
+
+    def partial_copy(step, d):
+        k = step * (rows - 1) + d - 1
+        return remote(partial.at[step, lax.rem(z + d, rows)], partial_in.at[step, d - 1],
+                      p_send.at[k], p_recv.at[k], (lax.rem(z + d, rows), c))
+
+    def block_of(step, i):
+        return solved.at[step, i // 2, lax.rem(i, 2)]
+
+    def spread_copy(step, d):
+        k = step * (rows - 1) + d - 1
+        return remote(block_of(step, z), block_of(step, z),
+                      b_send.at[k], b_recv.at[k], (lax.rem(z + d, rows), c))
+
+    def exchange(step):
+        return [
+            remote(solved.at[step, 1 - y], other_y.at[step],
+                   e_send.at[2 * step], e_recv.at[2 * step], (z, by_y)),
+            remote(solved.at[step, :, 1 - x], other_x.at[step],
+                   e_send.at[2 * step + 1], e_recv.at[2 * step + 1], (z, by_x)),
+        ]
+
+    def multiply_out(step):
+        b_high, b_low = split(acc[step])
+        for d in reversed(range(rows)):
+            @pl.when(z + d < rows)
+            def _():
+                i = z + d
+                a = inv[step, pl.ds(pl.multiple_of(i * tile, tile), tile), :]
+                partial[step, i] = product(*split(a), b_high, b_low)
+                if d:
+                    partial_copy(step, d).start()
+
+    def collect(step):
+        for d in range(1, rows):
+            @pl.when(z - d >= 0)
+            def _():
+                partial_copy(step, d).wait_recv()
+                partial[step, z] += partial_in[step, d - 1]
+        solved[step, z // 2, lax.rem(z, 2)] = partial[step, z]
+        for d in range(1, rows):
+            spread_copy(step, d).start()
+
+    def finish_solve(step):
+        for d in range(1, rows):
+            spread_copy(step, d).wait_recv()
+        for copy in exchange(step):
+            copy.start()
+        for k in range(2):
+            at = pl.ds(k * tile, tile)
+            for path, mine in enumerate((solved[step, y, k], solved[step, k, x])):
+                op_high[step, path, at, :lanes], op_low[step, path, at, :lanes] = split(mine)
+
+    def finish_exchange(step):
+        for path, (copy, other) in enumerate(zip(exchange(step), (other_y, other_x))):
+            copy.wait_recv()
+            for k in range(2):
+                at = pl.ds(k * tile, tile)
+                op_high[step, path, at, lanes:], op_low[step, path, at, lanes:] = split(
+                    other[step, k])
+
+    def fold(ref, k, step, path):
+        a = jnp.concatenate([ref[k, s] for s in range(4)], axis=1)
+        return product(*split(a), op_high[step, path], op_low[step, path])
+
+    def share(b, along_x):
+        return remote(outgoing.at[b], incoming.at[b], r_send.at[b], r_recv.at[b],
+                      (z, by_y if along_x else by_x))
+
+    def write_out(b):
+        return pltpu.make_async_copy(acc.at[b], sides_out.at[b], w_sem.at[b])
+
+    load_zero.wait()
+    load_inv1.wait()
+    multiply_out(0)
+    start_gathers(0, STAGE[0])
+    for copy in to_sibling[1:]:
+        copy.start()
+    write_out(0).start()
+    head.wait_recv()
+    head_forward.start()
+    collect(0)
+    start_gathers(STAGE[0], STAGE[1])
+    finish_solve(0)
+    pass_on(0, STAGE[2])
+    load_rest.wait()
+    own[0].wait()
+    to_sibling[0].wait_recv()
+    head_forward.wait_recv()
+    finish_exchange(0)
+
+    both = fold(c1, 0, 0, 0)
+    outgoing[1] = both[:, lanes:]
+    share(1, True).start()
+    acc[1] -= both[:, :lanes]
+    start_gathers(STAGE[1], STAGE[3])
+    load_inv2.wait()
+    share(1, True).wait_recv()
+    acc[1] -= incoming[1]
+    multiply_out(1)
+    write_out(1).start()
+    start_gathers(STAGE[3], pairs)
+    collect(1)
+    for copy in own[1:]:
+        copy.wait()
+    for copy in to_sibling[1:]:
+        copy.wait_recv()
+    finish_solve(1)
+    pass_on(STAGE[2], pairs)
+    finish_exchange(1)
+    store_solved = pltpu.make_async_copy(solved, solved_out, share_in.at[0])
+    store_solved.start()
+
+    @pl.loop(0, pairs)
+    def _(p):
+        for copy in forward_pair(p):
+            copy.wait_recv()
+        for path in range(2):
+            q = path * pairs + p
+            b = 2 + q
+            both = fold(c1, 1 + q, 0, path) + fold(c2, q, 1, path)
+            outgoing[b] = both[:, lanes:]
+            share(b, path == 0).start()
+            acc[b] -= both[:, :lanes]
+
+    @pl.loop(0, pairs)
+    def _(p):
+        for path in range(2):
+            b = 2 + path * pairs + p
+            share(b, path == 0).wait_recv()
+            acc[b] -= incoming[b]
+            write_out(b).start()
+
+    head.wait_send()
+    head_forward.wait_send()
+    share(1, True).wait_send()
+    for copy in to_sibling:
+        copy.wait_send()
+    for step in range(2):
+        for d in range(1, rows):
+            @pl.when(z + d < rows)
+            def _():
+                partial_copy(step, d).wait_send()
+            spread_copy(step, d).wait_send()
+        for copy in exchange(step):
+            copy.wait_send()
+    store_solved.wait()
+    write_out(0).wait()
+    write_out(1).wait()
+
+    @pl.loop(0, pairs)
+    def _(p):
+        for copy in gather_pair(p) + forward_pair(p):
+            copy.wait_send()
+        for path in range(2):
+            b = 2 + path * pairs + p
+            share(b, path == 0).wait_send()
+            write_out(b).wait()
+
+
+STAGE = (2, 4, 3, 5)
+
+
+def fused(rows, cols, sides, inv_one, inv_two, c_one, c_two):
+    nb, tile, lanes = sides.shape
+    n = inv_one.shape[0]
+    chunks = c_one.shape[0] + c_two.shape[0]
+    dma = pltpu.SemaphoreType.DMA
+    anywhere = pl.BlockSpec(memory_space=pl.ANY)
+    solved, updated = pl.pallas_call(
+        functools.partial(kernel, rows, cols),
+        out_shape=(
+            jax.ShapeDtypeStruct((2, 2, 2, tile, lanes), F32),
+            jax.ShapeDtypeStruct(sides.shape, F32),
+        ),
+        in_specs=[anywhere] * 5,
+        out_specs=(anywhere, anywhere),
+        scratch_shapes=[
+            pltpu.VMEM((nb, tile, lanes), F32),
+            pltpu.VMEM((2, n, tile), F32),
+            pltpu.VMEM((nb - 1, 4, tile, lanes), F32),
+            pltpu.VMEM((nb - 2, 4, tile, lanes), F32),
+            pltpu.VMEM((2, rows, tile, lanes), F32),
+            pltpu.VMEM((2, rows - 1, tile, lanes), F32),
+            pltpu.VMEM((2, 2, 2, tile, lanes), F32),
+            pltpu.VMEM((2, 2, tile, lanes), F32),
+            pltpu.VMEM((2, 2, tile, lanes), F32),
+            pltpu.VMEM((2, 2, 2 * tile, 2 * lanes), BF16),
+            pltpu.VMEM((2, 2, 2 * tile, 2 * lanes), BF16),
+            pltpu.VMEM((nb, tile, lanes), F32),
+            pltpu.VMEM((nb, tile, lanes), F32),
+            dma((1,)),
+            dma((9,)),
+            dma((chunks,)), dma((chunks,)),
+            dma((chunks,)), dma((chunks,)),
+            dma((5,)), dma((5,)),
+            dma((2 * (rows - 1),)), dma((2 * (rows - 1),)),
+            dma((2 * (rows - 1),)), dma((2 * (rows - 1),)),
+            dma((4,)), dma((4,)),
+            dma((nb,)), dma((nb,)),
+            dma((nb,)),
+        ],
+        compiler_params=pltpu.CompilerParams(
+            collective_id=0, has_side_effects=True, vmem_limit_bytes=48 * 2**20),
+        cost_estimate=pl.CostEstimate(
+            flops=6 * chunks * tile * n * lanes, bytes_accessed=16 * 2**20, transcendentals=0),
+    )(sides, inv_one, inv_two, c_one, c_two)
+    return solved.reshape(2, n, lanes), updated
 
 
 def apply_inverse(inverse, rhs_block):
@@ -41,8 +364,10 @@
         P(None, "row", "col"),
         P(None, "row", "col"),
     )
+    rows, cols = mesh.shape["row"], mesh.shape["col"]
+    local = functools.partial(fused, rows, cols) if (rows, cols) == (4, 8) else on_device
     return jax.shard_map(
-        on_device,
+        local,
         mesh=mesh,
         in_specs=placed,
         out_specs=(P(None, None, "col"), P(None, "row", "col")),

time: 221 us -> 104 us (0.47)
  waiting for transfers between devices: 150 us -> 0 us
  Pallas kernels: 0 us -> 95.6 us
  matrix products: 44.5 us -> 0 us
  between operations: 15.6 us -> 0.66 us
  other arithmetic: 2.37 us -> 0 us
    all_gather x2 -> x0, waiting for transfers between devices: 114 us -> none  [update_rows(): lax.all_gather(factor_panel, 'col', axis=2, tiled=True)]
    pallas_call x0 -> x1, Pallas kernels: none -> 95.6 us  [fused(): pl.pallas_call(functools.partial(kernel, rows, cols), out_shape=(jax.Shap...]
    dot_general x4 -> x0, matrix products: 44.5 us -> none  [the longest x2 40.1 us: fold_panel(): jnp.einsum('bij,jr->bir', fragment, solved, precision=HIGHEST, preferred_...]
    psum x2 -> x0, waiting for transfers between devices: 35 us -> none  [apply_inverse(): return lax.psum(local_product, 'row')]
    unnamed x7 -> x10, local copies, waits for them, and re-layouts: 4.86 us -> 7.22 us
    another operation x1 -> x0, other arithmetic: 2.24 us -> none  [on_device(): solutions = jnp.stack([solved_first, solved_second])]
  transfers between devices with their start and end apart: 4 -> 0, of which waited for: 3 -> 0; matrix products, arithmetic and copies ran while one was open for 11% -> 0% of each run, Pallas kernels for 0% -> 0%
where the time goes in v1:
time: 104 us; the launch traced here: 103 us
  Pallas kernels  95.6 us (92%)
  local copies, waits for them, and re-layouts  7.22 us (7%)
    pallas_call x1, Pallas kernels, fused(): pl.pallas_call(functools.partial(kernel, rows, cols), out_shape=(jax.Shap...  95.6 us
    unnamed x10, local copies, waits for them, and re-layouts  7.22 us

profile of v1, /device:TPU:8, one launch (start us, length us, event | category | flops | bytes accessed | tf_op | source)
XLA Modules:
  0.0 103.5 jit_solution(888940923820810909)
XLA Ops:
  0.6 0.0 copy-start
  0.6 1.5 %copy-done = f32[14,256,128]{2,1,0:T(8,128)S(1)} copy-done((f32[14,256,128]{2,1,0:T(8,128)S(1)}, f32[14,256,128]{2,1,0:T(8,128)}, u32[]{:S(2)}) %copy-start) | copy-done | bytes 1835032
  2.1 0.0 copy-start.1
  2.1 1.2 %copy-done.1 = f32[1024,256]{1,0:T(8,128)S(1)} copy-done((f32[1024,256]{1,0:T(8,128)S(1)}, f32[1024,256]{1,0:T(8,128)}, u32[]{:S(2)}) %copy-start.1) | copy-done | bytes 1048600
  3.4 0.0 copy-start.2
  3.4 1.2 %copy-done.2 = f32[1024,256]{1,0:T(8,128)S(1)} copy-done((f32[1024,256]{1,0:T(8,128)S(1)}, f32[1024,256]{1,0:T(8,128)}, u32[]{:S(2)}) %copy-start.2) | copy-done | bytes 1048600
  4.6 95.6 %shard_map.68 = (f32[2,2,2,256,128]{4,3,2,1,0:T(8,128)S(1)}, f32[16,256,128]{2,1,0:T(8,128)}) custom-call(f32[16,256,128]{2,1,0:T(8,128)} %sides.1, f32[1024,256]{1,0:T(8,128)S(1)} %copy-done.1, f32[1024,256]{1,0:T(8,128)S(1)} %copy-done.2, f32[15,256,128]{2,1,0:T(8,128)} %c_one.1, f32[14,256,128]{2,1,0:T(8,128)S(1)} %copy-done), custom_call_target="tpu_custom_call" | custom-call | flops 5838471168 | bytes 16777216 | tf_op jit(solution)/shard_map/pallas_call | solution.py:291
  100.2 0.0 copy-start.3
  100.2 1.0 copy.9
  101.2 1.0 copy-done.3
  102.2 1.3 %copy.10 = f32[16,256,128]{2,1,0:T(8,128)} copy(f32[16,256,128]{2,1,0:T(8,128)S(1)} %copy-done.3) | data formatting | bytes 4194304
Async XLA Ops:
  0.6 1.5 %copy-start = (f32[14,256,128]{2,1,0:T(8,128)S(1)}, f32[14,256,128]{2,1,0:T(8,128)}, u32[]{:S(2)}) copy-start(f32[14,256,128]{2,1,0:T(8,128)} %c_two.1) | copy-start | bytes 5505028
  2.1 1.2 %copy-start.1 = (f32[1024,256]{1,0:T(8,128)S(1)}, f32[1024,256]{1,0:T(8,128)}, u32[]{:S(2)}) copy-start(f32[1024,256]{1,0:T(8,128)} %inv_one.1) | copy-start | bytes 3145732
  3.4 1.2 %copy-start.2 = (f32[1024,256]{1,0:T(8,128)S(1)}, f32[1024,256]{1,0:T(8,128)}, u32[]{:S(2)}) copy-start(f32[1024,256]{1,0:T(8,128)} %inv_two.1) | copy-start | bytes 3145732
  100.2 2.0 %copy-start.3 = (f32[16,256,128]{2,1,0:T(8,128)S(1)}, f32[16,256,128]{2,1,0:T(8,128)}, u32[]{:S(2)}) copy-start(f32[16,256,128]{2,1,0:T(8,128)} %get-tuple-element.9) | copy-start | bytes 6291460

commit v2 on v1

--- a/solution.py
+++ b/solution.py
@@ -17,6 +17,10 @@
     high = value.astype(BF16)
     low = (value - high.astype(F32)).astype(BF16)
     return high, low
+
+
+def rows_of(i, n):
+    return pl.ds(pl.multiple_of(i * n, n), n)
 
 
 def product(a_high, a_low, b_high, b_low):
@@ -31,7 +35,7 @@
     acc, inv, c1, c2, partial, partial_in, solved, other_x, other_y,
     op_high, op_low, outgoing, incoming, share_in,
     local_sem, g_send, g_recv, f_send, f_recv, o_send, o_recv,
-    p_send, p_recv, b_send, b_recv, e_send, e_recv, r_send, r_recv, w_sem,
+    p_send, p_recv, up_send, down_send, b_recv, e_send, e_recv, r_send, r_recv, w_sem,
 ):
     nb, tile, lanes = sides.shape
     pairs = (nb - 2) // 2
@@ -120,63 +124,96 @@
     head.start()
     to_sibling[0].start()
 
-    def partial_copy(step, d):
-        k = step * (rows - 1) + d - 1
-        return remote(partial.at[step, lax.rem(z + d, rows)], partial_in.at[step, d - 1],
-                      p_send.at[k], p_recv.at[k], (lax.rem(z + d, rows), c))
+    def sum_copy(step, i):
+        k = step * rows + i
+        return remote(partial.at[step, i], partial_in.at[step, i],
+                      p_send.at[k], p_recv.at[k], (lax.rem(z + 1, rows), c))
 
     def block_of(step, i):
         return solved.at[step, i // 2, lax.rem(i, 2)]
 
-    def spread_copy(step, d):
-        k = step * (rows - 1) + d - 1
-        return remote(block_of(step, z), block_of(step, z),
-                      b_send.at[k], b_recv.at[k], (lax.rem(z + d, rows), c))
-
-    def exchange(step):
-        return [
-            remote(solved.at[step, 1 - y], other_y.at[step],
-                   e_send.at[2 * step], e_recv.at[2 * step], (z, by_y)),
-            remote(solved.at[step, :, 1 - x], other_x.at[step],
-                   e_send.at[2 * step + 1], e_recv.at[2 * step + 1], (z, by_x)),
-        ]
-
-    def multiply_out(step):
+    def up_copy(step, i):
+        k = step * rows + i
+        return remote(block_of(step, i), block_of(step, i), up_send.at[k], b_recv.at[k],
+                      (lax.rem(z + 1, rows), c))
+
+    def down_copy(step, to):
+        k = step * rows + z
+        return remote(block_of(step, z), block_of(step, z), down_send.at[step * rows + to],
+                      b_recv.at[k], (to, c))
+
+    def exchange_y(step, k):
+        at = 4 * step + k
+        return remote(solved.at[step, 1 - y, k], other_y.at[step, k],
+                      e_send.at[at], e_recv.at[at], (z, by_y))
+
+    def exchange_x(step, k):
+        at = 4 * step + 2 + k
+        return remote(solved.at[step, k, 1 - x], other_x.at[step, k],
+                      e_send.at[at], e_recv.at[at], (z, by_x))
+
+    def pass_block(step, i):
+        @pl.when(i // 2 == 1 - y)
+        def _():
+            exchange_y(step, lax.rem(i, 2)).start()
+
+        @pl.when(lax.rem(i, 2) == 1 - x)
+        def _():
+            exchange_x(step, i // 2).start()
+
+    def solve(step):
         b_high, b_low = split(acc[step])
-        for d in reversed(range(rows)):
-            @pl.when(z + d < rows)
-            def _():
-                i = z + d
-                a = inv[step, pl.ds(pl.multiple_of(i * tile, tile), tile), :]
+        for i in reversed(range(rows)):
+            @pl.when(z <= i)
+            def _():
+                a = inv[step, pl.ds(i * tile, tile), :]
                 partial[step, i] = product(*split(a), b_high, b_low)
-                if d:
-                    partial_copy(step, d).start()
-
-    def collect(step):
-        for d in range(1, rows):
-            @pl.when(z - d >= 0)
-            def _():
-                partial_copy(step, d).wait_recv()
-                partial[step, z] += partial_in[step, d - 1]
-        solved[step, z // 2, lax.rem(z, 2)] = partial[step, z]
-        for d in range(1, rows):
-            spread_copy(step, d).start()
-
-    def finish_solve(step):
-        for d in range(1, rows):
-            spread_copy(step, d).wait_recv()
-        for copy in exchange(step):
-            copy.start()
+
+                @pl.when(z > 0)
+                def _():
+                    sum_copy(step, i).wait_recv()
+                    partial[step, i] += partial_in[step, i]
+
+            if i:
+                @pl.when(z < i)
+                def _():
+                    sum_copy(step, i).start()
+
+            @pl.when(z == i)
+            def _():
+                solved[step, i // 2, i % 2] = partial[step, i]
+                for to in range(i):
+                    down_copy(step, to).start()
+
+            @pl.when(z > i)
+            def _():
+                up_copy(step, i).wait_recv()
+
+            if i < rows - 1:
+                @pl.when((z >= i) & (z < rows - 1))
+                def _():
+                    up_copy(step, i).start()
+
+            @pl.when(z >= i)
+            def _():
+                pass_block(step, i)
+
+    def finish_spread(step):
+        for i in range(1, rows):
+            @pl.when(z < i)
+            def _():
+                up_copy(step, i).wait_recv()
+                pass_block(step, i)
         for k in range(2):
             at = pl.ds(k * tile, tile)
             for path, mine in enumerate((solved[step, y, k], solved[step, k, x])):
                 op_high[step, path, at, :lanes], op_low[step, path, at, :lanes] = split(mine)
 
     def finish_exchange(step):
-        for path, (copy, other) in enumerate(zip(exchange(step), (other_y, other_x))):
-            copy.wait_recv()
+        for path, (copy, other) in enumerate(((exchange_y, other_y), (exchange_x, other_x))):
             for k in range(2):
                 at = pl.ds(k * tile, tile)
+                copy(step, k).wait_recv()
                 op_high[step, path, at, lanes:], op_low[step, path, at, lanes:] = split(
                     other[step, k])
 
@@ -193,17 +230,16 @@
 
     load_zero.wait()
     load_inv1.wait()
-    multiply_out(0)
     start_gathers(0, STAGE[0])
     for copy in to_sibling[1:]:
         copy.start()
     write_out(0).start()
+    solve(0)
+    finish_spread(0)
+    start_gathers(STAGE[0], STAGE[1])
+    pass_on(0, STAGE[2])
     head.wait_recv()
     head_forward.start()
-    collect(0)
-    start_gathers(STAGE[0], STAGE[1])
-    finish_solve(0)
-    pass_on(0, STAGE[2])
     load_rest.wait()
     own[0].wait()
     to_sibling[0].wait_recv()
@@ -218,15 +254,15 @@
     load_inv2.wait()
     share(1, True).wait_recv()
     acc[1] -= incoming[1]
-    multiply_out(1)
+    start_gathers(STAGE[3], STAGE[4])
+    solve(1)
     write_out(1).start()
-    start_gathers(STAGE[3], pairs)
-    collect(1)
     for copy in own[1:]:
         copy.wait()
     for copy in to_sibling[1:]:
         copy.wait_recv()
-    finish_solve(1)
+    finish_spread(1)
+    start_gathers(STAGE[4], pairs)
     pass_on(STAGE[2], pairs)
     finish_exchange(1)
     store_solved = pltpu.make_async_copy(solved, solved_out, share_in.at[0])
@@ -258,13 +294,22 @@
     for copy in to_sibling:
         copy.wait_send()
     for step in range(2):
-        for d in range(1, rows):
-            @pl.when(z + d < rows)
-            def _():
-                partial_copy(step, d).wait_send()
-            spread_copy(step, d).wait_send()
-        for copy in exchange(step):
-            copy.wait_send()
+        for i in range(rows):
+            @pl.when(z < i)
+            def _():
+                sum_copy(step, i).wait_send()
+
+            @pl.when((z >= i) & (z < rows - 1))
+            def _():
+                up_copy(step, i).wait_send()
+
+            @pl.when(z > i)
+            def _():
+                down_copy(step, i).wait_send()
+
+        for k in range(2):
+            exchange_y(step, k).wait_send()
+            exchange_x(step, k).wait_send()
     store_solved.wait()
     write_out(0).wait()
     write_out(1).wait()
@@ -279,7 +324,7 @@
             write_out(b).wait()
 
 
-STAGE = (2, 4, 3, 5)
+STAGE = (3, 4, 2, 4, 7)
 
 
 def fused(rows, cols, sides, inv_one, inv_two, c_one, c_two):
@@ -302,7 +347,7 @@
             pltpu.VMEM((nb - 1, 4, tile, lanes), F32),
             pltpu.VMEM((nb - 2, 4, tile, lanes), F32),
             pltpu.VMEM((2, rows, tile, lanes), F32),
-            pltpu.VMEM((2, rows - 1, tile, lanes), F32),
+            pltpu.VMEM((2, rows, tile, lanes), F32),
             pltpu.VMEM((2, 2, 2, tile, lanes), F32),
             pltpu.VMEM((2, 2, tile, lanes), F32),
             pltpu.VMEM((2, 2, tile, lanes), F32),
@@ -315,14 +360,14 @@
             dma((chunks,)), dma((chunks,)),
             dma((chunks,)), dma((chunks,)),
             dma((5,)), dma((5,)),
-            dma((2 * (rows - 1),)), dma((2 * (rows - 1),)),
-            dma((2 * (rows - 1),)), dma((2 * (rows - 1),)),
-            dma((4,)), dma((4,)),
+            dma((2 * rows,)), dma((2 * rows,)),
+            dma((2 * rows,)), dma((2 * rows,)), dma((2 * rows,)),
+            dma((8,)), dma((8,)),
             dma((nb,)), dma((nb,)),
             dma((nb,)),
         ],
         compiler_params=pltpu.CompilerParams(
-            collective_id=0, has_side_effects=True, vmem_limit_bytes=48 * 2**20),
+            collective_id=0, has_side_effects=True, vmem_limit_bytes=60 * 2**20),
         cost_estimate=pl.CostEstimate(
             flops=6 * chunks * tile * n * lanes, bytes_accessed=16 * 2**20, transcendentals=0),
     )(sides, inv_one, inv_two, c_one, c_two)

time: 104 us -> 94.2 us (0.906)
  Pallas kernels: 95.6 us -> 88.9 us
  local copies, waits for them, and re-layouts: 7.22 us -> 3.73 us
    pallas_call x1, Pallas kernels: 95.6 us -> 88.9 us  [fused(): pl.pallas_call(functools.partial(kernel, rows, cols), out_shape=(jax.Shap...]
    unnamed x10 -> x4, local copies, waits for them, and re-layouts: 7.22 us -> 3.73 us
where the time goes in v2:
time: 94.2 us; the launch traced here: 93.3 us
  Pallas kernels  88.9 us (94%)
  local copies, waits for them, and re-layouts  3.73 us (4%)
    pallas_call x1, Pallas kernels, fused(): pl.pallas_call(functools.partial(kernel, rows, cols), out_shape=(jax.Shap...  88.9 us
    unnamed x4, local copies, waits for them, and re-layouts  3.73 us

profile of v2, /device:TPU:8, one launch (start us, length us, event | category | flops | bytes accessed | tf_op | source)
XLA Modules:
  0.0 93.3 jit_solution(8079774725375370963)
XLA Ops:
  0.6 88.9 %shard_map.68 = (f32[2,2,2,256,128]{4,3,2,1,0:T(8,128)}, f32[16,256,128]{2,1,0:T(8,128)}) custom-call(f32[16,256,128]{2,1,0:T(8,128)} %sides.1, f32[1024,256]{1,0:T(8,128)} %inv_one.1, f32[1024,256]{1,0:T(8,128)} %inv_two.1, f32[15,256,128]{2,1,0:T(8,128)} %c_one.1, f32[14,256,128]{2,1,0:T(8,128)} %c_two.1), custom_call_target="tpu_custom_call" | custom-call | flops 5838471168 | bytes 16777216 | tf_op jit(solution)/shard_map/pallas_call | solution.py:336
  89.6 0.0 copy-start
  89.6 2.4 %copy.9 = f32[2,1024,128]{2,1,0:T(8,128)} copy(f32[2,1024,128]{2,1,0:T(8,128)} %bitcast.1) | data formatting | bytes 2097152
  92.0 0.0 copy-done
  92.0 1.3 %copy.10 = f32[16,256,128]{2,1,0:T(8,128)} copy(f32[16,256,128]{2,1,0:T(8,128)S(1)} %copy-done) | data formatting | bytes 4194304
Async XLA Ops:
  89.6 2.4 %copy-start = (f32[16,256,128]{2,1,0:T(8,128)S(1)}, f32[16,256,128]{2,1,0:T(8,128)}, u32[]{:S(2)}) copy-start(f32[16,256,128]{2,1,0:T(8,128)} %get-tuple-element.9) | copy-start | bytes 6291460

commit v3 on v2

--- a/solution.py
+++ b/solution.py
@@ -124,98 +124,106 @@
     head.start()
     to_sibling[0].start()
 
-    def sum_copy(step, i):
-        k = step * rows + i
-        return remote(partial.at[step, i], partial_in.at[step, i],
+    half = tile // 2
+    pieces = 2 * rows
+
+    def sum_copy(step, j):
+        k = step * pieces + j
+        return remote(partial.at[step, j], partial_in.at[step, j],
                       p_send.at[k], p_recv.at[k], (lax.rem(z + 1, rows), c))
 
-    def block_of(step, i):
-        return solved.at[step, i // 2, lax.rem(i, 2)]
-
-    def up_copy(step, i):
-        k = step * rows + i
-        return remote(block_of(step, i), block_of(step, i), up_send.at[k], b_recv.at[k],
+    def piece_of(step, j):
+        return solved.at[step, j // 4, j // 2 % 2, j % 2]
+
+    def up_copy(step, j):
+        k = step * pieces + j
+        return remote(piece_of(step, j), piece_of(step, j), up_send.at[k], b_recv.at[k],
                       (lax.rem(z + 1, rows), c))
 
-    def down_copy(step, to):
-        k = step * rows + z
-        return remote(block_of(step, z), block_of(step, z), down_send.at[step * rows + to],
+    def down_copy(step, j, to):
+        k = step * pieces + j
+        return remote(piece_of(step, j), piece_of(step, j), down_send.at[k * rows + to],
                       b_recv.at[k], (to, c))
 
-    def exchange_y(step, k):
-        at = 4 * step + k
-        return remote(solved.at[step, 1 - y, k], other_y.at[step, k],
+    def exchange_y(step, k, part):
+        at = 8 * step + 2 * k + part
+        return remote(solved.at[step, 1 - y, k, part], other_y.at[step, k, part],
                       e_send.at[at], e_recv.at[at], (z, by_y))
 
-    def exchange_x(step, k):
-        at = 4 * step + 2 + k
-        return remote(solved.at[step, k, 1 - x], other_x.at[step, k],
+    def exchange_x(step, k, part):
+        at = 8 * step + 4 + 2 * k + part
+        return remote(solved.at[step, k, 1 - x, part], other_x.at[step, k, part],
                       e_send.at[at], e_recv.at[at], (z, by_x))
 
-    def pass_block(step, i):
-        @pl.when(i // 2 == 1 - y)
+    def pass_piece(step, j):
+        @pl.when(y == 1 - j // 4)
         def _():
-            exchange_y(step, lax.rem(i, 2)).start()
-
-        @pl.when(lax.rem(i, 2) == 1 - x)
+            exchange_y(step, j // 2 % 2, j % 2).start()
+
+        @pl.when(x == 1 - j // 2 % 2)
         def _():
-            exchange_x(step, i // 2).start()
+            exchange_x(step, j // 4, j % 2).start()
 
     def solve(step):
         b_high, b_low = split(acc[step])
-        for i in reversed(range(rows)):
-            @pl.when(z <= i)
-            def _():
-                a = inv[step, pl.ds(i * tile, tile), :]
-                partial[step, i] = product(*split(a), b_high, b_low)
+        for j in reversed(range(pieces)):
+            holder = j // 2
+
+            @pl.when(z <= holder)
+            def _():
+                a = inv[step, pl.ds(j * half, half), :]
+                partial[step, j] = product(*split(a), b_high, b_low)
 
                 @pl.when(z > 0)
                 def _():
-                    sum_copy(step, i).wait_recv()
-                    partial[step, i] += partial_in[step, i]
-
-            if i:
+                    sum_copy(step, j).wait_recv()
+                    partial[step, j] += partial_in[step, j]
+
+            if holder:
+                @pl.when(z < holder)
+                def _():
+                    sum_copy(step, j).start()
+
+            @pl.when(z == holder)
+            def _():
+                solved[step, j // 4, j // 2 % 2, j % 2] = partial[step, j]
+                for to in range(holder):
+                    down_copy(step, j, to).start()
+
+            @pl.when(z > holder)
+            def _():
+                up_copy(step, j).wait_recv()
+
+            if holder < rows - 1:
+                @pl.when((z >= holder) & (z < rows - 1))
+                def _():
+                    up_copy(step, j).start()
+
+            @pl.when(z >= holder)
+            def _():
+                pass_piece(step, j)
+
+    def finish_spread(step):
+        for i in range(1, rows):
+            for j in (2 * i + 1, 2 * i):
                 @pl.when(z < i)
                 def _():
-                    sum_copy(step, i).start()
-
-            @pl.when(z == i)
-            def _():
-                solved[step, i // 2, i % 2] = partial[step, i]
-                for to in range(i):
-                    down_copy(step, to).start()
-
-            @pl.when(z > i)
-            def _():
-                up_copy(step, i).wait_recv()
-
-            if i < rows - 1:
-                @pl.when((z >= i) & (z < rows - 1))
-                def _():
-                    up_copy(step, i).start()
-
-            @pl.when(z >= i)
-            def _():
-                pass_block(step, i)
-
-    def finish_spread(step):
-        for i in range(1, rows):
-            @pl.when(z < i)
-            def _():
-                up_copy(step, i).wait_recv()
-                pass_block(step, i)
+                    up_copy(step, j).wait_recv()
+                    pass_piece(step, j)
         for k in range(2):
             at = pl.ds(k * tile, tile)
             for path, mine in enumerate((solved[step, y, k], solved[step, k, x])):
-                op_high[step, path, at, :lanes], op_low[step, path, at, :lanes] = split(mine)
+                op_high[step, path, at, :lanes], op_low[step, path, at, :lanes] = split(
+                    mine.reshape(tile, lanes))
 
     def finish_exchange(step):
         for path, (copy, other) in enumerate(((exchange_y, other_y), (exchange_x, other_x))):
             for k in range(2):
                 at = pl.ds(k * tile, tile)
-                copy(step, k).wait_recv()
+                copy(step, k, 1).wait_recv()
+                copy(step, k, 0).wait_recv()
                 op_high[step, path, at, lanes:], op_low[step, path, at, lanes:] = split(
-                    other[step, k])
+                    other[step, k].reshape(tile, lanes))
 
     def fold(ref, k, step, path):
         a = jnp.concatenate([ref[k, s] for s in range(4)], axis=1)
@@ -294,22 +302,26 @@
     for copy in to_sibling:
         copy.wait_send()
     for step in range(2):
-        for i in range(rows):
-            @pl.when(z < i)
-            def _():
-                sum_copy(step, i).wait_send()
-
-            @pl.when((z >= i) & (z < rows - 1))
-            def _():
-                up_copy(step, i).wait_send()
-
-            @pl.when(z > i)
-            def _():
-                down_copy(step, i).wait_send()
+        for j in range(pieces):
+            holder = j // 2
+
+            @pl.when(z < holder)
+            def _():
+                sum_copy(step, j).wait_send()
+
+            @pl.when((z >= holder) & (z < rows - 1))
+            def _():
+                up_copy(step, j).wait_send()
+
+            @pl.when(z == holder)
+            def _():
+                for to in range(holder):
+                    down_copy(step, j, to).wait_send()
 
         for k in range(2):
-            exchange_y(step, k).wait_send()
-            exchange_x(step, k).wait_send()
+            for part in range(2):
+                exchange_y(step, k, part).wait_send()
+                exchange_x(step, k, part).wait_send()
     store_solved.wait()
     write_out(0).wait()
     write_out(1).wait()
@@ -336,7 +348,7 @@
     solved, updated = pl.pallas_call(
         functools.partial(kernel, rows, cols),
         out_shape=(
-            jax.ShapeDtypeStruct((2, 2, 2, tile, lanes), F32),
+            jax.ShapeDtypeStruct((2, 2, 2, 2, tile // 2, lanes), F32),
             jax.ShapeDtypeStruct(sides.shape, F32),
         ),
         in_specs=[anywhere] * 5,
@@ -346,11 +358,11 @@
             pltpu.VMEM((2, n, tile), F32),
             pltpu.VMEM((nb - 1, 4, tile, lanes), F32),
             pltpu.VMEM((nb - 2, 4, tile, lanes), F32),
-            pltpu.VMEM((2, rows, tile, lanes), F32),
-            pltpu.VMEM((2, rows, tile, lanes), F32),
-            pltpu.VMEM((2, 2, 2, tile, lanes), F32),
-            pltpu.VMEM((2, 2, tile, lanes), F32),
-            pltpu.VMEM((2, 2, tile, lanes), F32),
+            pltpu.VMEM((2, 2 * rows, tile // 2, lanes), F32),
+            pltpu.VMEM((2, 2 * rows, tile // 2, lanes), F32),
+            pltpu.VMEM((2, 2, 2, 2, tile // 2, lanes), F32),
+            pltpu.VMEM((2, 2, 2, tile // 2, lanes), F32),
+            pltpu.VMEM((2, 2, 2, tile // 2, lanes), F32),
             pltpu.VMEM((2, 2, 2 * tile, 2 * lanes), BF16),
             pltpu.VMEM((2, 2, 2 * tile, 2 * lanes), BF16),
             pltpu.VMEM((nb, tile, lanes), F32),
@@ -360,9 +372,9 @@
             dma((chunks,)), dma((chunks,)),
             dma((chunks,)), dma((chunks,)),
             dma((5,)), dma((5,)),
-            dma((2 * rows,)), dma((2 * rows,)),
-            dma((2 * rows,)), dma((2 * rows,)), dma((2 * rows,)),
-            dma((8,)), dma((8,)),
+            dma((4 * rows,)), dma((4 * rows,)),
+            dma((4 * rows,)), dma((4 * rows * rows,)), dma((4 * rows,)),
+            dma((16,)), dma((16,)),
             dma((nb,)), dma((nb,)),
             dma((nb,)),
         ],

time: 94.2 us -> 92.2 us (0.979)
  Pallas kernels: 88.9 us -> 87.7 us
    pallas_call x1, Pallas kernels: 88.9 us -> 87.7 us  [fused(): pl.pallas_call(functools.partial(kernel, rows, cols), out_shape=(jax.Shap...]
where the time goes in v3:
time: 92.2 us; the launch traced here: 92 us
  Pallas kernels  87.7 us (95%)
  local copies, waits for them, and re-layouts  3.73 us (4%)
    pallas_call x1, Pallas kernels, fused(): pl.pallas_call(functools.partial(kernel, rows, cols), out_shape=(jax.Shap...  87.7 us
    unnamed x4, local copies, waits for them, and re-layouts  3.73 us

profile of v3, /device:TPU:8, one launch (start us, length us, event | category | flops | bytes accessed | tf_op | source)
XLA Modules:
  0.0 92.0 jit_solution(2512843043254650548)
XLA Ops:
  0.6 87.7 %shard_map.68 = (f32[2,2,2,2,128,128]{5,4,3,2,1,0:T(8,128)}, f32[16,256,128]{2,1,0:T(8,128)}) custom-call(f32[16,256,128]{2,1,0:T(8,128)} %sides.1, f32[1024,256]{1,0:T(8,128)} %inv_one.1, f32[1024,256]{1,0:T(8,128)} %inv_two.1, f32[15,256,128]{2,1,0:T(8,128)} %c_one.1, f32[14,256,128]{2,1,0:T(8,128)} %c_two.1), custom_call_target="tpu_custom_call" | custom-call | flops 5838471168 | bytes 16777216 | tf_op jit(solution)/shard_map/pallas_call | solution.py:348
  88.3 0.0 copy-start
  88.3 2.4 %copy.9 = f32[2,1024,128]{2,1,0:T(8,128)} copy(f32[2,1024,128]{2,1,0:T(8,128)} %bitcast.1) | data formatting | bytes 2097152
  90.7 0.0 copy-done
  90.7 1.3 %copy.10 = f32[16,256,128]{2,1,0:T(8,128)} copy(f32[16,256,128]{2,1,0:T(8,128)S(1)} %copy-done) | data formatting | bytes 4194304
Async XLA Ops:
  88.3 2.4 %copy-start = (f32[16,256,128]{2,1,0:T(8,128)S(1)}, f32[16,256,128]{2,1,0:T(8,128)}, u32[]{:S(2)}) copy-start(f32[16,256,128]{2,1,0:T(8,128)} %get-tuple-element.9) | copy-start | bytes 6291460
